TPU v7x, 32 devices: a whole 2x2x4 slice. The times are simulated.
32 devices in a mesh: ctx: 32 (over z, y, x, core), tp: 1.
Axes of the slice: x: 2, y: 2, z: 4, core: 2. Of those that a mesh axis runs over, the one named last changes fastest.
Arguments:
- query_in: bfloat16 [8192, 2048], P('ctx', 'tp'), may hold values from -6 to 6
- key_in: bfloat16 [8192, 2048], P('ctx', 'tp'), may hold values from -6 to 6
- value_in: bfloat16 [8192, 4096], P('ctx', 'tp'), may hold values from -6 to 6
- gate_values: bfloat16 [8192, 4096], P('ctx', 'tp'), may hold values from -6 to 6
- query_conv: bfloat16 [4, 2048], P(None, 'tp'), may hold values from -3 to 3
- key_conv: bfloat16 [4, 2048], P(None, 'tp'), may hold values from -3 to 3
- value_conv: bfloat16 [4, 4096], P(None, 'tp'), may hold values from -3 to 3
- beta_rate: float32 [32, 8192], P('tp', 'ctx'), may hold values from 0.002 to 0.9, as said below
- log_decay: float32 [32, 8192], P('tp', 'ctx'), may hold values from -0.8 to 0, as said below
- norm_gain: float32 [128], replicated, may hold values from 0.1 to 1.9
- out_weight: bfloat16 [4096, 2048], P('tp'), may hold values from -0.09375 to 0.09375
Outputs:
- layer_out: bfloat16 [8192, 2048], P(('ctx', 'tp'))
Inputs may be any that keep to these rules, and one draw needn't show every extreme that they name: beta_rate lies strictly between 0 and 1. log_decay is never positive.
All inputs are finite; a program needn't handle non-finite values.
Results may differ from a plain program's by a relative error of at most 0.014.
Values may be sent and summed in bfloat16 or wider, within the bound.
A program may use at most 256 MiB of HBM per device.

v0:
```python
import functools
import math

import jax
import jax.numpy as jnp
from jax import lax
from jax.experimental import pallas as pl
from jax.experimental.pallas import tpu as pltpu
from jax.sharding import PartitionSpec as P

HK = 16
HV = 32
DK = 128
DV = 128
SUB = 128
RIM = 16
EXTRA = 16
MESH = pl.DeviceIdType.MESH
f32 = jnp.float32
bf16 = jnp.bfloat16


def mm(a, b):
    return jnp.dot(a.astype(bf16), b.astype(bf16), preferred_element_type=f32)


def split(a):
    high = a.astype(bf16)
    return high, (a - high.astype(f32)).astype(bf16)


def silu(x):
    return x / (1.0 + jnp.exp(-x))


def conv(raw_ref, rim, taps_ref, lo, hi):
    rows = raw_ref.shape[0]
    joined = jnp.concatenate([rim[RIM // 2 :, lo:hi], raw_ref[:, lo:hi].astype(f32)], axis=0)
    taps = taps_ref[:, lo:hi].astype(f32)
    count = taps.shape[0]
    first = RIM // 2 - count + 1
    total = taps[0:1] * joined[first : first + rows]
    for j in range(1, count):
        total = total + taps[j : j + 1] * joined[first + j : first + j + rows]
    return silu(total)


def running_sums(decay):
    rows = decay.shape[1]
    row = lax.broadcasted_iota(jnp.int32, (rows, rows), 0)
    col = lax.broadcasted_iota(jnp.int32, (rows, rows), 1)
    ones = (row <= col).astype(f32).astype(bf16)
    high, rest = split(decay)
    middle, low = split(decay - high.astype(f32))
    return mm(high, ones) + (mm(middle, ones) + mm(low, ones))


def unit_lower_inverses(lowers):
    size = lowers[0].shape[0]
    row = lax.broadcasted_iota(jnp.int32, (size, size), 0)
    col = lax.broadcasted_iota(jnp.int32, (size, size), 1)
    eye = (row == col).astype(f32)
    pair = ((row // 2) == (col // 2)) & (row != col)
    found = [eye - jnp.where(pair, low, 0.0) for low in lowers]
    step = 2
    while step < size:
        take = ((row // (2 * step)) == (col // (2 * step))) & ((row // step) != (col // step))
        halves = [x.astype(bf16) for x in found]
        first = [mm(jnp.where(take, low, 0.0), x) for low, x in zip(lowers, halves)]
        found = [f - mm(x, y) for f, x, y in zip(found, halves, first)]
        step *= 2
    return [x.astype(bf16) for x in found]


def layer_kernel(
    n1, n2, key_heads, ratio, hb,
    q_ref, k_ref, v_ref, qtap, ktap, vtap, beta_ref, decay_ref, gain_ref,
    q_hbm, k_hbm, v_hbm, gate_hbm, weight_hbm, out_ref,
    rates, rim, gate, weight, emitted, probing, msg, got, pre_m, pre_s, pre_a, start, ready, back, starting, gated,
    rim_send, rim_recv, load_sem, send_sem, recv_sem, chain_send, chain_recv, back_send, back_recv,
):
    step = pl.program_id(0)
    steps = pl.num_programs(0)
    me = lax.axis_index("ctx")
    tp = lax.axis_index("tp")
    total_devices = n1 * n2
    plane = me // n1
    place = me % n1
    base = plane * n1
    first, last = plane == 0, plane == n2 - 1
    rows = q_ref.shape[0]
    q_cols, v_cols = q_hbm.shape[1], v_hbm.shape[1]
    heads = key_heads * ratio
    per_step = heads // hb

    def at(index):
        return (index, tp)

    rim_cols = ((q_hbm, 0, q_cols), (k_hbm, q_cols, q_cols), (v_hbm, 2 * q_cols, v_cols))
    rim_copies = [
        pltpu.make_async_remote_copy(
            src_ref=source.at[pl.ds(rows - RIM, RIM)],
            dst_ref=rim.at[:, pl.ds(offset, width)],
            send_sem=rim_send.at[i],
            recv_sem=rim_recv.at[i],
            device_id=at((me + 1) % total_devices),
            device_id_type=MESH,
        )
        for i, (source, offset, width) in enumerate(rim_cols)
    ]
    weight_copy = pltpu.make_async_copy(weight_hbm, weight, load_sem.at[0])
    gate_copy = pltpu.make_async_copy(gate_hbm, gate, load_sem.at[1])

    @pl.when(step == 0)
    def _():
        barrier = pltpu.get_barrier_semaphore()

        def greet(index):
            pl.semaphore_signal(barrier, inc=1, device_id=at(index), device_id_type=MESH)

        partners = n1 - 1 + jnp.where(first, 0, 1) + jnp.where(last, 0, 1)
        for d in range(1, n1):
            greet(base + (place + d) % n1)

        @pl.when(jnp.logical_not(first))
        def _():
            greet(me - n1)

        @pl.when(jnp.logical_not(last))
        def _():
            greet(me + n1)

        if n1 > 1:
            before = jnp.logical_and(place == 0, me > 0)
            after = jnp.logical_and(place == n1 - 1, me < total_devices - 1)
            partners = partners + jnp.where(before, 1, 0) + jnp.where(after, 1, 0)

            @pl.when(before)
            def _():
                greet(me - 1)

            @pl.when(after)
            def _():
                greet(me + 1)

        pl.semaphore_wait(barrier, partners)

        @pl.when(me < total_devices - 1)
        def _():
            for copy in rim_copies:
                copy.start()

        gate_copy.start()
        weight_copy.start()
        sums = running_sums(decay_ref[...])
        for g in range(rates.shape[0]):
            rates[g, 0:heads] = sums[g * heads : (g + 1) * heads]
            rates[g, heads : 2 * heads] = beta_ref[g * heads : (g + 1) * heads, :]

        @pl.when(me == 0)
        def _():
            rim[...] = jnp.zeros_like(rim)

        @pl.when(me > 0)
        def _():
            for copy in rim_copies:
                copy.wait_recv()

    local_rates = rates[step]
    rate_cols = local_rates.T
    key_width, value_width = key_heads * DK, heads * DV

    def rim_part(offset, width):
        return rim[:, pl.ds(pl.multiple_of(offset + step * width, DK), width)].astype(f32)

    q_rim = rim_part(0, key_width)
    k_rim = rim_part(q_cols, key_width)
    v_rim = rim_part(2 * q_cols, value_width)
    row = lax.broadcasted_iota(jnp.int32, (rows, rows), 0)
    col = lax.broadcasted_iota(jnp.int32, (rows, rows), 1)
    sub = min(SUB, rows)
    count = rows // sub
    lowers, sims, rights, probes, tails, totals = [], [], [], [], [], []
    for g in range(key_heads):
        lo, hi = g * DK, (g + 1) * DK
        q = conv(q_ref, q_rim, qtap, lo, hi)
        k = conv(k_ref, k_rim, ktap, lo, hi)
        k = k * lax.rsqrt(jnp.sum(k * k, axis=-1, keepdims=True) + 1e-06)
        k_turned = k.T
        k_right = k_turned.astype(bf16)
        kk = mm(k, k_right)
        qk = mm(q, k_right)
        for r in range(ratio):
            h = g * ratio + r
            v = conv(v_ref, v_rim, vtap, h * DV, (h + 1) * DV)
            cum = rate_cols[:, h : h + 1]
            beta = rate_cols[:, heads + h : heads + h + 1]
            cum_row = local_rates[h : h + 1]
            fade = jnp.exp(jnp.minimum(cum - cum_row, 0.0))
            lowers.append(jnp.where(row > col, beta * fade * kk, 0.0))
            sims.append(jnp.where(row >= col, fade * qk, 0.0).astype(bf16))
            grown = jnp.exp(cum)
            rights.append(jnp.concatenate([beta * v, (beta * grown) * k], axis=1))
            probes.append(grown * q)
            end = cum_row[:, rows - 1 : rows]
            tails.append((k_turned * jnp.exp(end - cum_row)).astype(bf16))
            totals.append(jnp.exp(end))
    pieces = [
        low[i * sub : (i + 1) * sub, i * sub : (i + 1) * sub] for low in lowers for i in range(count)
    ]
    inverses = unit_lower_inverses(pieces)
    upper = lax.broadcasted_iota(jnp.int32, (EXTRA, DV), 0) < EXTRA // 2
    for h in range(heads):
        low = lowers[h]
        solved = []
        for i in range(count):
            right = rights[h][i * sub : (i + 1) * sub]
            if i > 0:
                before = jnp.concatenate(solved, axis=0)
                right = right - mm(low[i * sub : (i + 1) * sub, : i * sub], before)
            solved.append(mm(inverses[h * count + i], right).astype(bf16))
        solved = jnp.concatenate(solved, axis=0)
        seen = mm(sims[h], solved)
        lanes = pl.ds(pl.multiple_of((step * heads + h) * DV, DV), DV)
        emitted[:, lanes] = seen[:, :DV]
        probing[:, lanes] = (probes[h] - seen[:, DV:]).astype(bf16)
        update = mm(tails[h], solved)
        at_head = step * heads + h
        msg[at_head, 0:DK, :] = update[:, DV:].astype(bf16)
        msg[at_head, DK : 2 * DK, :] = update[:, :DV].astype(bf16)
        high, rest = split(jnp.broadcast_to(totals[h], (EXTRA, DV)))
        msg[at_head, 2 * DK :, :] = jnp.where(upper, high.astype(f32), rest.astype(f32)).astype(bf16)

    def map_copy(peer):
        return pltpu.make_async_remote_copy(
            src_ref=msg.at[pl.ds(peer * hb, hb)],
            dst_ref=got.at[place],
            send_sem=send_sem.at[peer],
            recv_sem=recv_sem.at[place],
            device_id=at(base + peer),
            device_id_type=MESH,
        )

    for j in range(per_step):
        peer = step * per_step + j

        @pl.when(peer != place)
        def _():
            map_copy(peer).start()

        @pl.when(peer == place)
        def _():
            pltpu.make_async_copy(
                msg.at[pl.ds(peer * hb, hb)], got.at[place], recv_sem.at[place]
            ).start()

    @pl.when(step == steps - 1)
    def _():
        maps = [jnp.zeros((DK, DK), f32) for _ in range(hb)]
        states = [jnp.zeros((DK, DV), f32) for _ in range(hb)]
        fades = [jnp.ones((1, DV), f32) for _ in range(hb)]
        eye_row = lax.broadcasted_iota(jnp.int32, (DK, DK), 0)
        eye_col = lax.broadcasted_iota(jnp.int32, (DK, DK), 1)
        eye = (eye_row == eye_col).astype(f32)
        for i in range(n1):
            pltpu.make_async_copy(got.at[i], got.at[i], recv_sem.at[i]).wait()
            for h in range(hb):
                pre_m[i, h] = maps[h].astype(bf16)
                pre_s[i, h] = states[h]
                pre_a[i, h] = jnp.broadcast_to(fades[h], (8, DV))
                m = got[i, h, 0:DK, :]
                s = got[i, h, DK : 2 * DK, :].astype(f32)
                tail = got[i, h, 2 * DK : 2 * DK + EXTRA, :].astype(f32)
                a = tail[0:1] + tail[EXTRA // 2 : EXTRA // 2 + 1]
                both = mm(m, jnp.concatenate([fades[h] * eye - maps[h], states[h]], axis=1))
                maps[h] = a * maps[h] + both[:, :DK]
                states[h] = a * states[h] - both[:, DK:] + s
                fades[h] = a * fades[h]

        @pl.when(first)
        def _():
            for h in range(hb):
                start[h] = jnp.zeros((DK, DV), bf16)

        chain = pltpu.make_async_remote_copy(
            src_ref=ready,
            dst_ref=start,
            send_sem=chain_send,
            recv_sem=chain_recv,
            device_id=at((me + n1) % total_devices),
            device_id_type=MESH,
        )

        @pl.when(jnp.logical_not(first))
        def _():
            chain.wait_recv()

        @pl.when(jnp.logical_not(last))
        def _():
            for h in range(hb):
                begin = start[h]
                ready[h] = (
                    fades[h] * begin.astype(f32) - mm(maps[h], begin) + states[h]
                ).astype(bf16)
            chain.start()

        for i in range(n1):
            for h in range(hb):
                begin = start[h]
                back[i, h] = (
                    pre_a[i, h, 0:1] * begin.astype(f32) - mm(pre_m[i, h], begin) + pre_s[i, h]
                ).astype(bf16)

        mine = pl.ds(place * hb, hb)
        returned = []
        for d in range(1, n1):
            peer = (place + d) % n1
            copy = pltpu.make_async_remote_copy(
                src_ref=back.at[peer],
                dst_ref=starting.at[mine],
                send_sem=back_send.at[d],
                recv_sem=back_recv.at[place],
                device_id=at(base + peer),
                device_id_type=MESH,
            )
            copy.start()
            returned.append(copy)
        pltpu.make_async_copy(back.at[place], starting.at[mine], back_recv.at[place]).start()
        gate_copy.wait()
        gain = gain_ref[...]
        for i in range(n1):
            part = starting.at[pl.ds(i * hb, hb)]
            pltpu.make_async_copy(part, part, back_recv.at[i]).wait()
            for h in range(i * hb, (i + 1) * hb):
                lo, hi = h * DV, (h + 1) * DV
                core = emitted[:, lo:hi] + mm(probing[:, lo:hi], starting[h])
                scale = lax.rsqrt(jnp.mean(core * core, axis=-1, keepdims=True) + 1e-06)
                gated[:, lo:hi] = (
                    core * scale * gain * silu(gate[:, lo:hi].astype(f32))
                ).astype(bf16)
        weight_copy.wait()
        width = out_ref.shape[1]
        tile = math.gcd(width, 512)

        def project(t, carry):
            lanes = pl.ds(pl.multiple_of(t * tile, tile), tile)
            out_ref[:, lanes] = jnp.dot(
                gated[...], weight[:, lanes], preferred_element_type=f32
            ).astype(bf16)
            return carry

        lax.fori_loop(0, width // tile, project, 0)
        for copy in returned:
            copy.wait_send()
        for peer in range(n1):
            @pl.when(peer != place)
            def _():
                map_copy(peer).wait_send()

        @pl.when(jnp.logical_not(last))
        def _():
            chain.wait_send()

        @pl.when(me < total_devices - 1)
        def _():
            for copy in rim_copies:
                copy.wait_send()


def layer(n_ctx, query, key, value, gate, taps, beta, decay, gain, weight):
    rows, q_cols = query.shape
    v_cols = value.shape[1]
    key_heads, value_heads = q_cols // DK, v_cols // DV
    ratio = value_heads // key_heads
    n1 = math.gcd(math.gcd(value_heads, n_ctx), 8)
    n2 = n_ctx // n1
    hb = value_heads // n1
    step = math.gcd(key_heads, 2)
    while (step * ratio) % hb:
        step *= 2
    groups = key_heads // step
    heads = step * ratio
    kw, vw = step * DK, heads * DV
    width = weight.shape[1]
    wide = lambda n, size: pl.BlockSpec((n, size), lambda g: (0, g))
    whole = lambda shape: pl.BlockSpec(shape, lambda g: (0, 0))
    anywhere = pl.BlockSpec(memory_space=pl.ANY)
    count = taps[0].shape[0]
    return pl.pallas_call(
        functools.partial(layer_kernel, n1, n2, step, ratio, hb),
        grid=(groups,),
        in_specs=[
            wide(rows, kw), wide(rows, kw), wide(rows, vw),
            wide(count, kw), wide(count, kw), wide(count, vw),
            whole(beta.shape), whole(decay.shape), whole((1, DV)),
            anywhere, anywhere, anywhere, anywhere, anywhere,
        ],
        out_specs=whole((rows, width)),
        out_shape=jax.ShapeDtypeStruct((rows, width), bf16),
        scratch_shapes=[
            pltpu.VMEM((groups, 2 * heads, rows), f32),
            pltpu.VMEM((RIM, 2 * q_cols + v_cols), bf16),
            pltpu.VMEM(gate.shape, bf16),
            pltpu.VMEM(weight.shape, bf16),
            pltpu.VMEM((rows, v_cols), f32),
            pltpu.VMEM((rows, v_cols), bf16),
            pltpu.VMEM((value_heads, 2 * DK + EXTRA, DV), bf16),
            pltpu.VMEM((n1, hb, 2 * DK + EXTRA, DV), bf16),
            pltpu.VMEM((n1, hb, DK, DK), bf16),
            pltpu.VMEM((n1, hb, DK, DV), f32),
            pltpu.VMEM((n1, hb, 8, DV), f32),
            pltpu.VMEM((hb, DK, DV), bf16),
            pltpu.VMEM((hb, DK, DV), bf16),
            pltpu.VMEM((n1, hb, DK, DV), bf16),
            pltpu.VMEM((value_heads, DK, DV), bf16),
            pltpu.VMEM((rows, v_cols), bf16),
            pltpu.SemaphoreType.DMA((3,)),
            pltpu.SemaphoreType.DMA((3,)),
            pltpu.SemaphoreType.DMA((2,)),
            pltpu.SemaphoreType.DMA((n1,)),
            pltpu.SemaphoreType.DMA((n1,)),
            pltpu.SemaphoreType.DMA,
            pltpu.SemaphoreType.DMA,
            pltpu.SemaphoreType.DMA((n1,)),
            pltpu.SemaphoreType.DMA((n1,)),
        ],
        compiler_params=pltpu.CompilerParams(
            collective_id=0, has_side_effects=True, vmem_limit_bytes=60 << 20
        ),
        name="layer",
    )(
        query, key, value, *taps, beta, decay, gain.reshape(1, DV),
        query, key, value, gate, weight,
    )


def local(
    n_ctx, n_tp,
    query_in, key_in, value_in, gate_values, query_conv, key_conv, value_conv,
    beta_rate, log_decay, norm_gain, out_weight,
):
    partial = layer(
        n_ctx, query_in, key_in, value_in, gate_values, (query_conv, key_conv, value_conv),
        beta_rate, log_decay, norm_gain, out_weight,
    )
    if n_tp == 1:
        return partial
    return lax.psum_scatter(partial, "tp", scatter_dimension=0, tiled=True)


def solution(mesh):
    return jax.shard_map(
        functools.partial(local, mesh.shape["ctx"], mesh.shape["tp"]),
        mesh=mesh,
        in_specs=(
            P("ctx", "tp"), P("ctx", "tp"), P("ctx", "tp"), P("ctx", "tp"),
            P(None, "tp"), P(None, "tp"), P(None, "tp"),
            P("tp", "ctx"), P("tp", "ctx"), P(), P("tp", None),
        ),
        out_specs=P(("ctx", "tp"), None),
        check_vma=False,
    )
```

profile of v0, /device:TPU:29, one launch (start us, length us, event | category | flops | bytes accessed | tf_op | source)
XLA Modules:
  0.0 98.8 jit_solution(9386331460674148623)
XLA Ops:
  0.0 96.5 %layer.1 = bf16[256,2048]{1,0:T(8,128)(2,1)} custom-call(bf16[256,2048]{1,0:T(8,128)(2,1)} %q_hbm.1, bf16[256,2048]{1,0:T(8,128)(2,1)} %k_hbm.1, bf16[256,4096]{1,0:T(8,128)(2,1)} %v_hbm.1, bf16[4,2048]{1,0:T(4,128)(2,1)} %qtap.1, bf16[4,2048]{1,0:T(4,128)(2,1)} %ktap.1, bf16[4,4096]{1,0:T(4,128)(2,1)} %vtap.1, f32[32,256]{1,0:T(8,128)} %beta_ref.1, ...), custom_call_target="tpu_custom_call" | custom-call | tf_op jit(solution)/shard_map/layer/pallas_call | solution.py:389
  96.5 2.3 %copy.13 = bf16[256,2048]{1,0:T(8,128)(2,1)} copy(bf16[256,2048]{1,0:T(8,128)(2,1)} %layer.1) | data formatting | bytes 2097152
where the time goes:
time: 99 us; the launch traced here: 98.8 us
  Pallas kernels  96.5 us (97%)
  local copies, waits for them, and re-layouts  2.3 us (2%)
    pallas_call x1, Pallas kernels, layer(): pl.pallas_call(functools.partial(layer_kernel, n1, n2, step, ratio, hb),...  96.5 us
    unnamed x1, local copies, waits for them, and re-layouts  2.3 us

commit v1 on v0

--- a/solution.py
+++ b/solution.py
@@ -76,7 +76,7 @@
     n1, n2, key_heads, ratio, hb,
     q_ref, k_ref, v_ref, qtap, ktap, vtap, beta_ref, decay_ref, gain_ref,
     q_hbm, k_hbm, v_hbm, gate_hbm, weight_hbm, out_ref,
-    rates, rim, gate, weight, emitted, probing, msg, got, pre_m, pre_s, pre_a, start, ready, back, starting, gated,
+    rates, rim, gate, weight, emitted, probing, msg, got, pre_m, pre_s, pre_a, start, ready, back, starting, gated, acc,
     rim_send, rim_recv, load_sem, send_sem, recv_sem, chain_send, chain_recv, back_send, back_recv,
 ):
     step = pl.program_id(0)
@@ -254,7 +254,62 @@
                 msg.at[pl.ds(peer * hb, hb)], got.at[place], recv_sem.at[place]
             ).start()
 
-    @pl.when(step == steps - 1)
+    turn = jnp.minimum(place // per_step + 2 + plane, steps - 1)
+    late = jnp.logical_and(place == n1 - 1, 2 * plane >= n2)
+
+    def chain_copy(h):
+        return pltpu.make_async_remote_copy(
+            src_ref=ready.at[h],
+            dst_ref=start.at[h],
+            send_sem=chain_send.at[h],
+            recv_sem=chain_recv.at[h],
+            device_id=at((me + n1) % total_devices),
+            device_id_type=MESH,
+        )
+
+    def back_copy(d):
+        return pltpu.make_async_remote_copy(
+            src_ref=back.at[(place + d) % n1],
+            dst_ref=starting.at[pl.ds(place * hb, hb)],
+            send_sem=back_send.at[d],
+            recv_sem=back_recv.at[place],
+            device_id=at(base + (place + d) % n1),
+            device_id_type=MESH,
+        )
+
+    def advance(i, h, begin):
+        return (
+            pre_a[i, h, 0:1] * begin.astype(f32) - mm(pre_m[i, h], begin) + pre_s[i, h]
+        ).astype(bf16)
+
+    def chain_and_return():
+        @pl.when(first)
+        def _():
+            for h in range(hb):
+                start[h] = jnp.zeros((DK, DV), bf16)
+
+        for h in range(hb):
+            @pl.when(jnp.logical_not(first))
+            def _():
+                chain_copy(h).wait_recv()
+
+            @pl.when(jnp.logical_not(last))
+            def _():
+                ready[h] = advance(n1, h, start[h])
+                chain_copy(h).start()
+
+        for d in range(1, n1):
+            peer = (place + d) % n1
+            for h in range(hb):
+                back[peer, h] = advance(peer, h, start[h])
+            back_copy(d).start()
+        for h in range(hb):
+            back[place, h] = advance(place, h, start[h])
+        pltpu.make_async_copy(
+            back.at[place], starting.at[pl.ds(place * hb, hb)], back_recv.at[place]
+        ).start()
+
+    @pl.when(step == turn)
     def _():
         maps = [jnp.zeros((DK, DK), f32) for _ in range(hb)]
         states = [jnp.zeros((DK, DV), f32) for _ in range(hb)]
@@ -262,12 +317,15 @@
         eye_row = lax.broadcasted_iota(jnp.int32, (DK, DK), 0)
         eye_col = lax.broadcasted_iota(jnp.int32, (DK, DK), 1)
         eye = (eye_row == eye_col).astype(f32)
-        for i in range(n1):
-            pltpu.make_async_copy(got.at[i], got.at[i], recv_sem.at[i]).wait()
+        for i in range(n1 + 1):
             for h in range(hb):
                 pre_m[i, h] = maps[h].astype(bf16)
                 pre_s[i, h] = states[h]
                 pre_a[i, h] = jnp.broadcast_to(fades[h], (8, DV))
+            if i == n1:
+                break
+            pltpu.make_async_copy(got.at[i], got.at[i], recv_sem.at[i]).wait()
+            for h in range(hb):
                 m = got[i, h, 0:DK, :]
                 s = got[i, h, DK : 2 * DK, :].astype(f32)
                 tail = got[i, h, 2 * DK : 2 * DK + EXTRA, :].astype(f32)
@@ -277,58 +335,18 @@
                 states[h] = a * states[h] - both[:, DK:] + s
                 fades[h] = a * fades[h]
 
-        @pl.when(first)
-        def _():
-            for h in range(hb):
-                start[h] = jnp.zeros((DK, DV), bf16)
-
-        chain = pltpu.make_async_remote_copy(
-            src_ref=ready,
-            dst_ref=start,
-            send_sem=chain_send,
-            recv_sem=chain_recv,
-            device_id=at((me + n1) % total_devices),
-            device_id_type=MESH,
-        )
-
-        @pl.when(jnp.logical_not(first))
-        def _():
-            chain.wait_recv()
-
-        @pl.when(jnp.logical_not(last))
-        def _():
-            for h in range(hb):
-                begin = start[h]
-                ready[h] = (
-                    fades[h] * begin.astype(f32) - mm(maps[h], begin) + states[h]
-                ).astype(bf16)
-            chain.start()
-
-        for i in range(n1):
-            for h in range(hb):
-                begin = start[h]
-                back[i, h] = (
-                    pre_a[i, h, 0:1] * begin.astype(f32) - mm(pre_m[i, h], begin) + pre_s[i, h]
-                ).astype(bf16)
-
-        mine = pl.ds(place * hb, hb)
-        returned = []
-        for d in range(1, n1):
-            peer = (place + d) % n1
-            copy = pltpu.make_async_remote_copy(
-                src_ref=back.at[peer],
-                dst_ref=starting.at[mine],
-                send_sem=back_send.at[d],
-                recv_sem=back_recv.at[place],
-                device_id=at(base + peer),
-                device_id_type=MESH,
-            )
-            copy.start()
-            returned.append(copy)
-        pltpu.make_async_copy(back.at[place], starting.at[mine], back_recv.at[place]).start()
-        gate_copy.wait()
+        @pl.when(jnp.logical_not(late))
+        def _():
+            chain_and_return()
+
+    @pl.when(step == steps - 1)
+    def _():
         gain = gain_ref[...]
-        for i in range(n1):
+        width = out_ref.shape[1]
+        tile = math.gcd(width, 512)
+        early = (n1 - 1) * hb * DV
+
+        def gate_heads(i):
             part = starting.at[pl.ds(i * hb, hb)]
             pltpu.make_async_copy(part, part, back_recv.at[i]).wait()
             for h in range(i * hb, (i + 1) * hb):
@@ -338,20 +356,38 @@
                 gated[:, lo:hi] = (
                     core * scale * gain * silu(gate[:, lo:hi].astype(f32))
                 ).astype(bf16)
+
+        gate_copy.wait()
+        for i in range(n1 - 1):
+            gate_heads(i)
+
+        @pl.when(late)
+        def _():
+            chain_and_return()
+
         weight_copy.wait()
-        width = out_ref.shape[1]
-        tile = math.gcd(width, 512)
-
-        def project(t, carry):
+
+        def project_early(t, carry):
             lanes = pl.ds(pl.multiple_of(t * tile, tile), tile)
-            out_ref[:, lanes] = jnp.dot(
-                gated[...], weight[:, lanes], preferred_element_type=f32
-            ).astype(bf16)
+            acc[:, lanes] = jnp.dot(
+                gated[:, :early], weight[:early, lanes], preferred_element_type=f32
+            )
             return carry
 
-        lax.fori_loop(0, width // tile, project, 0)
-        for copy in returned:
-            copy.wait_send()
+        def project_late(t, carry):
+            lanes = pl.ds(pl.multiple_of(t * tile, tile), tile)
+            total = jnp.dot(gated[:, early:], weight[early:, lanes], preferred_element_type=f32)
+            if early > 0:
+                total = total + acc[:, lanes]
+            out_ref[:, lanes] = total.astype(bf16)
+            return carry
+
+        if early > 0:
+            lax.fori_loop(0, width // tile, project_early, 0)
+        gate_heads(n1 - 1)
+        lax.fori_loop(0, width // tile, project_late, 0)
+        for d in range(1, n1):
+            back_copy(d).wait_send()
         for peer in range(n1):
             @pl.when(peer != place)
             def _():
@@ -359,7 +395,8 @@
 
         @pl.when(jnp.logical_not(last))
         def _():
-            chain.wait_send()
+            for h in range(hb):
+                chain_copy(h).wait_send()
 
         @pl.when(me < total_devices - 1)
         def _():
@@ -406,21 +443,22 @@
             pltpu.VMEM((rows, v_cols), bf16),
             pltpu.VMEM((value_heads, 2 * DK + EXTRA, DV), bf16),
             pltpu.VMEM((n1, hb, 2 * DK + EXTRA, DV), bf16),
-            pltpu.VMEM((n1, hb, DK, DK), bf16),
-            pltpu.VMEM((n1, hb, DK, DV), f32),
-            pltpu.VMEM((n1, hb, 8, DV), f32),
+            pltpu.VMEM((n1 + 1, hb, DK, DK), bf16),
+            pltpu.VMEM((n1 + 1, hb, DK, DV), f32),
+            pltpu.VMEM((n1 + 1, hb, 8, DV), f32),
             pltpu.VMEM((hb, DK, DV), bf16),
             pltpu.VMEM((hb, DK, DV), bf16),
             pltpu.VMEM((n1, hb, DK, DV), bf16),
             pltpu.VMEM((value_heads, DK, DV), bf16),
             pltpu.VMEM((rows, v_cols), bf16),
+            pltpu.VMEM((rows, width), f32),
             pltpu.SemaphoreType.DMA((3,)),
             pltpu.SemaphoreType.DMA((3,)),
             pltpu.SemaphoreType.DMA((2,)),
             pltpu.SemaphoreType.DMA((n1,)),
             pltpu.SemaphoreType.DMA((n1,)),
-            pltpu.SemaphoreType.DMA,
-            pltpu.SemaphoreType.DMA,
+            pltpu.SemaphoreType.DMA((hb,)),
+            pltpu.SemaphoreType.DMA((hb,)),
             pltpu.SemaphoreType.DMA((n1,)),
             pltpu.SemaphoreType.DMA((n1,)),
         ],

time: 99 us -> 108 us (1.091)
  Pallas kernels: 96.5 us -> 106 us
    pallas_call x1, Pallas kernels: 96.5 us -> 106 us  [layer(): pl.pallas_call(functools.partial(layer_kernel, n1, n2, step, ratio, hb),...]
where the time goes in v1:
time: 108 us
  Pallas kernels  106 us (98%)
  local copies, waits for them, and re-layouts  2.3 us (2%)
    pallas_call x1, Pallas kernels, layer(): pl.pallas_call(functools.partial(layer_kernel, n1, n2, step, ratio, hb),...  106 us
    unnamed x1, local copies, waits for them, and re-layouts  2.3 us

profile of v1, /device:TPU:29, one launch (start us, length us, event | category | flops | bytes accessed | tf_op | source)
XLA Modules:
  0.0 108.0 jit_solution(17725187513965791462)
XLA Ops:
  0.0 105.7 %layer.1 = bf16[256,2048]{1,0:T(8,128)(2,1)} custom-call(bf16[256,2048]{1,0:T(8,128)(2,1)} %q_hbm.1, bf16[256,2048]{1,0:T(8,128)(2,1)} %k_hbm.1, bf16[256,4096]{1,0:T(8,128)(2,1)} %v_hbm.1, bf16[4,2048]{1,0:T(4,128)(2,1)} %qtap.1, bf16[4,2048]{1,0:T(4,128)(2,1)} %ktap.1, bf16[4,4096]{1,0:T(4,128)(2,1)} %vtap.1, f32[32,256]{1,0:T(8,128)} %beta_ref.1, ...), custom_call_target="tpu_custom_call" | custom-call | tf_op jit(solution)/shard_map/layer/pallas_call | solution.py:426
  105.7 2.3 %copy.13 = bf16[256,2048]{1,0:T(8,128)(2,1)} copy(bf16[256,2048]{1,0:T(8,128)(2,1)} %layer.1) | data formatting | bytes 2097152

commit v2 on v0

--- a/solution.py
+++ b/solution.py
@@ -55,19 +55,46 @@
     return mm(high, ones) + (mm(middle, ones) + mm(low, ones))
 
 
+def odd_rows(x, step):
+    count = x.shape[0] // (2 * step)
+    return jnp.concatenate(
+        [x[(2 * j + 1) * step : (2 * j + 2) * step] for j in range(count)], axis=0
+    )
+
+
+def with_odd_rows(even, odd, step):
+    parts = []
+    for j in range(odd.shape[0] // step):
+        parts.append(even[2 * j * step : (2 * j + 1) * step])
+        parts.append(odd[j * step : (j + 1) * step])
+    return jnp.concatenate(parts, axis=0)
+
+
 def unit_lower_inverses(lowers):
     size = lowers[0].shape[0]
     row = lax.broadcasted_iota(jnp.int32, (size, size), 0)
     col = lax.broadcasted_iota(jnp.int32, (size, size), 1)
     eye = (row == col).astype(f32)
+    zero = jnp.zeros((size, size), f32)
     pair = ((row // 2) == (col // 2)) & (row != col)
     found = [eye - jnp.where(pair, low, 0.0) for low in lowers]
     step = 2
     while step < size:
-        take = ((row // (2 * step)) == (col // (2 * step))) & ((row // step) != (col // step))
         halves = [x.astype(bf16) for x in found]
-        first = [mm(jnp.where(take, low, 0.0), x) for low, x in zip(lowers, halves)]
-        found = [f - mm(x, y) for f, x, y in zip(found, halves, first)]
+        if step < 8:
+            take = ((row // (2 * step)) == (col // (2 * step))) & ((row // step) != (col // step))
+            first = [mm(jnp.where(take, low, 0.0), x) for low, x in zip(lowers, halves)]
+            found = [f - mm(x, y) for f, x, y in zip(found, halves, first)]
+        else:
+            half_row = lax.broadcasted_iota(jnp.int32, (size // 2, size), 0)
+            half_col = lax.broadcasted_iota(jnp.int32, (size // 2, size), 1)
+            take = (half_col // step) == 2 * (half_row // step)
+            first = [
+                mm(jnp.where(take, odd_rows(low, step), 0.0), x) for low, x in zip(lowers, halves)
+            ]
+            odds = [odd_rows(f, step) for f in found]
+            odds = [o - mm(o, with_odd_rows(zero, y, step)) for o, y in zip(odds, first)]
+            found = [with_odd_rows(f, o, step) for f, o in zip(found, odds)]
         step *= 2
     return [x.astype(bf16) for x in found]
 
@@ -76,7 +103,7 @@
     n1, n2, key_heads, ratio, hb,
     q_ref, k_ref, v_ref, qtap, ktap, vtap, beta_ref, decay_ref, gain_ref,
     q_hbm, k_hbm, v_hbm, gate_hbm, weight_hbm, out_ref,
-    rates, rim, gate, weight, emitted, probing, msg, got, pre_m, pre_s, pre_a, start, ready, back, starting, gated,
+    rates, rim, gate, weight, emitted, probing, msg, got, pre_m, pre_s, pre_a, start, ready, back, starting, gated, scaled,
     rim_send, rim_recv, load_sem, send_sem, recv_sem, chain_send, chain_recv, back_send, back_recv,
 ):
     step = pl.program_id(0)
@@ -282,27 +309,42 @@
             for h in range(hb):
                 start[h] = jnp.zeros((DK, DV), bf16)
 
-        chain = pltpu.make_async_remote_copy(
-            src_ref=ready,
-            dst_ref=start,
-            send_sem=chain_send,
-            recv_sem=chain_recv,
-            device_id=at((me + n1) % total_devices),
-            device_id_type=MESH,
-        )
-
-        @pl.when(jnp.logical_not(first))
-        def _():
-            chain.wait_recv()
-
-        @pl.when(jnp.logical_not(last))
-        def _():
-            for h in range(hb):
+        def chain_copy(h):
+            return pltpu.make_async_remote_copy(
+                src_ref=ready.at[h],
+                dst_ref=start.at[h],
+                send_sem=chain_send.at[h],
+                recv_sem=chain_recv.at[h],
+                device_id=at((me + n1) % total_devices),
+                device_id_type=MESH,
+            )
+
+        gain = gain_ref[...]
+
+        def gate_part(h, carry):
+            lanes = pl.ds(pl.multiple_of(h * DV, DV), DV)
+            scaled[:, lanes] = gain * silu(gate[:, lanes].astype(f32))
+            return carry
+
+        gate_copy.wait()
+        waits = 2 * plane >= n2
+
+        @pl.when(waits)
+        def _():
+            lax.fori_loop(0, n1 * hb, gate_part, 0)
+
+        for h in range(hb):
+            @pl.when(jnp.logical_not(first))
+            def _():
+                chain_copy(h).wait_recv()
+
+            @pl.when(jnp.logical_not(last))
+            def _():
                 begin = start[h]
                 ready[h] = (
                     fades[h] * begin.astype(f32) - mm(maps[h], begin) + states[h]
                 ).astype(bf16)
-            chain.start()
+                chain_copy(h).start()
 
         for i in range(n1):
             for h in range(hb):
@@ -326,8 +368,11 @@
             copy.start()
             returned.append(copy)
         pltpu.make_async_copy(back.at[place], starting.at[mine], back_recv.at[place]).start()
-        gate_copy.wait()
-        gain = gain_ref[...]
+
+        @pl.when(jnp.logical_not(waits))
+        def _():
+            lax.fori_loop(0, n1 * hb, gate_part, 0)
+
         for i in range(n1):
             part = starting.at[pl.ds(i * hb, hb)]
             pltpu.make_async_copy(part, part, back_recv.at[i]).wait()
@@ -335,9 +380,7 @@
                 lo, hi = h * DV, (h + 1) * DV
                 core = emitted[:, lo:hi] + mm(probing[:, lo:hi], starting[h])
                 scale = lax.rsqrt(jnp.mean(core * core, axis=-1, keepdims=True) + 1e-06)
-                gated[:, lo:hi] = (
-                    core * scale * gain * silu(gate[:, lo:hi].astype(f32))
-                ).astype(bf16)
+                gated[:, lo:hi] = (core * scale * scaled[:, lo:hi]).astype(bf16)
         weight_copy.wait()
         width = out_ref.shape[1]
         tile = math.gcd(width, 512)
@@ -359,7 +402,8 @@
 
         @pl.when(jnp.logical_not(last))
         def _():
-            chain.wait_send()
+            for h in range(hb):
+                chain_copy(h).wait_send()
 
         @pl.when(me < total_devices - 1)
         def _():
@@ -414,13 +458,14 @@
             pltpu.VMEM((n1, hb, DK, DV), bf16),
             pltpu.VMEM((value_heads, DK, DV), bf16),
             pltpu.VMEM((rows, v_cols), bf16),
+            pltpu.VMEM((rows, v_cols), f32),
             pltpu.SemaphoreType.DMA((3,)),
             pltpu.SemaphoreType.DMA((3,)),
             pltpu.SemaphoreType.DMA((2,)),
             pltpu.SemaphoreType.DMA((n1,)),
             pltpu.SemaphoreType.DMA((n1,)),
-            pltpu.SemaphoreType.DMA,
-            pltpu.SemaphoreType.DMA,
+            pltpu.SemaphoreType.DMA((hb,)),
+            pltpu.SemaphoreType.DMA((hb,)),
             pltpu.SemaphoreType.DMA((n1,)),
             pltpu.SemaphoreType.DMA((n1,)),
         ],

time: 99 us -> 96.1 us (0.971)
  Pallas kernels: 96.5 us -> 93.7 us
    pallas_call x1, Pallas kernels: 96.5 us -> 93.7 us  [layer(): pl.pallas_call(functools.partial(layer_kernel, n1, n2, step, ratio, hb),...]
where the time goes in v2:
time: 96.1 us; the launch traced here: 96 us
  Pallas kernels  93.7 us (98%)
  local copies, waits for them, and re-layouts  2.3 us (2%)
    pallas_call x1, Pallas kernels, layer(): pl.pallas_call(functools.partial(layer_kernel, n1, n2, step, ratio, hb),...  93.7 us
    unnamed x1, local copies, waits for them, and re-layouts  2.3 us

profile of v2, /device:TPU:29, one launch (start us, length us, event | category | flops | bytes accessed | tf_op | source)
XLA Modules:
  0.0 96.0 jit_solution(4627018428232684573)
XLA Ops:
  0.0 93.7 %layer.1 = bf16[256,2048]{1,0:T(8,128)(2,1)} custom-call(bf16[256,2048]{1,0:T(8,128)(2,1)} %q_hbm.1, bf16[256,2048]{1,0:T(8,128)(2,1)} %k_hbm.1, bf16[256,4096]{1,0:T(8,128)(2,1)} %v_hbm.1, bf16[4,2048]{1,0:T(4,128)(2,1)} %qtap.1, bf16[4,2048]{1,0:T(4,128)(2,1)} %ktap.1, bf16[4,4096]{1,0:T(4,128)(2,1)} %vtap.1, f32[32,256]{1,0:T(8,128)} %beta_ref.1, ...), custom_call_target="tpu_custom_call" | custom-call | tf_op jit(solution)/shard_map/layer/pallas_call | solution.py:433
  93.7 2.3 %copy.13 = bf16[256,2048]{1,0:T(8,128)(2,1)} copy(bf16[256,2048]{1,0:T(8,128)(2,1)} %layer.1) | data formatting | bytes 2097152

commit v3 on v2

--- a/solution.py
+++ b/solution.py
@@ -85,6 +85,15 @@
             take = ((row // (2 * step)) == (col // (2 * step))) & ((row // step) != (col // step))
             first = [mm(jnp.where(take, low, 0.0), x) for low, x in zip(lowers, halves)]
             found = [f - mm(x, y) for f, x, y in zip(found, halves, first)]
+        elif 2 * step == size:
+            first = [mm(low[step:, :step], x[:step, :step]) for low, x in zip(lowers, halves)]
+            corners = [mm(x[step:, step:], y) for x, y in zip(halves, first)]
+            found = [
+                jnp.concatenate(
+                    [f[:step], jnp.concatenate([-c, f[step:, step:]], axis=1)], axis=0
+                )
+                for f, c in zip(found, corners)
+            ]
         else:
             half_row = lax.broadcasted_iota(jnp.int32, (size // 2, size), 0)
             half_col = lax.broadcasted_iota(jnp.int32, (size // 2, size), 1)
@@ -419,7 +428,7 @@
     n1 = math.gcd(math.gcd(value_heads, n_ctx), 8)
     n2 = n_ctx // n1
     hb = value_heads // n1
-    step = math.gcd(key_heads, 2)
+    step = math.gcd(key_heads, 4)
     while (step * ratio) % hb:
         step *= 2
     groups = key_heads // step

time: 96.1 us -> 94.3 us (0.981)
  Pallas kernels: 93.7 us -> 91.8 us
    pallas_call x1, Pallas kernels: 93.7 us -> 91.8 us  [layer(): pl.pallas_call(functools.partial(layer_kernel, n1, n2, step, ratio, hb),...]
where the time goes in v3:
time: 94.3 us; the launch traced here: 94.1 us
  Pallas kernels  91.8 us (97%)
  local copies, waits for them, and re-layouts  2.3 us (2%)
    pallas_call x1, Pallas kernels, layer(): pl.pallas_call(functools.partial(layer_kernel, n1, n2, step, ratio, hb),...  91.8 us
    unnamed x1, local copies, waits for them, and re-layouts  2.3 us

profile of v3, /device:TPU:29, one launch (start us, length us, event | category | flops | bytes accessed | tf_op | source)
XLA Modules:
  0.0 94.1 jit_solution(17369214202659865673)
XLA Ops:
  0.0 91.8 %layer.1 = bf16[256,2048]{1,0:T(8,128)(2,1)} custom-call(bf16[256,2048]{1,0:T(8,128)(2,1)} %q_hbm.1, bf16[256,2048]{1,0:T(8,128)(2,1)} %k_hbm.1, bf16[256,4096]{1,0:T(8,128)(2,1)} %v_hbm.1, bf16[4,2048]{1,0:T(4,128)(2,1)} %qtap.1, bf16[4,2048]{1,0:T(4,128)(2,1)} %ktap.1, bf16[4,4096]{1,0:T(4,128)(2,1)} %vtap.1, f32[32,256]{1,0:T(8,128)} %beta_ref.1, ...), custom_call_target="tpu_custom_call" | custom-call | tf_op jit(solution)/shard_map/layer/pallas_call | solution.py:442
  91.8 2.3 %copy.13 = bf16[256,2048]{1,0:T(8,128)(2,1)} copy(bf16[256,2048]{1,0:T(8,128)(2,1)} %layer.1) | data formatting | bytes 2097152

commit v4 on v3

--- a/solution.py
+++ b/solution.py
@@ -30,7 +30,8 @@
 
 
 def silu(x):
-    return x / (1.0 + jnp.exp(-x))
+    half = 0.5 * x
+    return half + half * jnp.tanh(half)
 
 
 def conv(raw_ref, rim, taps_ref, lo, hi):

time: 94.3 us -> 94.2 us (level)
  no operation moved by 1% of the time
where the time goes in v4:
time: 94.2 us; the launch traced here: 94 us
  Pallas kernels  91.7 us (97%)
  local copies, waits for them, and re-layouts  2.3 us (2%)
    pallas_call x1, Pallas kernels, layer(): pl.pallas_call(functools.partial(layer_kernel, n1, n2, step, ratio, hb),...  91.7 us
    unnamed x1, local copies, waits for them, and re-layouts  2.3 us

profile of v4, /device:TPU:29, one launch (start us, length us, event | category | flops | bytes accessed | tf_op | source)
XLA Modules:
  0.0 94.0 jit_solution(1650813921307707802)
XLA Ops:
  0.0 91.7 %layer.1 = bf16[256,2048]{1,0:T(8,128)(2,1)} custom-call(bf16[256,2048]{1,0:T(8,128)(2,1)} %q_hbm.1, bf16[256,2048]{1,0:T(8,128)(2,1)} %k_hbm.1, bf16[256,4096]{1,0:T(8,128)(2,1)} %v_hbm.1, bf16[4,2048]{1,0:T(4,128)(2,1)} %qtap.1, bf16[4,2048]{1,0:T(4,128)(2,1)} %ktap.1, bf16[4,4096]{1,0:T(4,128)(2,1)} %vtap.1, f32[32,256]{1,0:T(8,128)} %beta_ref.1, ...), custom_call_target="tpu_custom_call" | custom-call | tf_op jit(solution)/shard_map/layer/pallas_call | solution.py:443
  91.7 2.3 %copy.13 = bf16[256,2048]{1,0:T(8,128)(2,1)} copy(bf16[256,2048]{1,0:T(8,128)(2,1)} %layer.1) | data formatting | bytes 2097152
